TPU v7x, 32 devices: a whole 2x2x4 slice. The times are simulated.
32 devices in a mesh: col: 8 (over z, x), row: 4 (over y, core).
Axes of the slice: x: 2, y: 2, z: 4, core: 2. Of those that a mesh axis runs over, the one named last changes fastest.
Arguments:
- jacobian: float32 [1024, 1024], P(('col', 'row')), may hold values from -6 to 6
- counts: int32 [1024], P(('col', 'row')), may hold values from 0 to 2
Outputs:
- factored: float32 [8, 4, 32, 1, 8, 128], P(None, 'row', None, None, 'col')
- r_rows: float32 [256, 1, 8, 128], P(None, None, 'col')
All inputs are finite; a program needn't handle non-finite values.
Results may differ from a plain program's by a relative error of at most 0.0003.
Values sent between devices are 32-bit elements; how exact they have to be, the bound alone decides.
A program may use at most 64 MiB of HBM per device.

v0:
```python
import math

import jax
import jax.numpy as jnp
from jax import lax
from jax.sharding import PartitionSpec as P

BLOCK = 128
PANELS = 2


HIGH = lax.Precision.HIGHEST


def from_root(value, axis, source):
    kept = jnp.where(lax.axis_index(axis) == source, value, 0).astype(value.dtype)
    return lax.psum(kept, axis)


def gram_of(block_cols):
    return jnp.dot(block_cols.T, block_cols, precision=HIGH, preferred_element_type=jnp.float32)


def complete(panel_cols, first_gram):
    lower_one = jnp.linalg.cholesky(first_gram)
    basis = jax.scipy.linalg.solve_triangular(lower_one, panel_cols.T, lower=True).T
    return (basis, lower_one.T)


def shards(jacobian, counts):
    rows_dev, width = jacobian.shape
    col_devices = lax.axis_size("col")
    slot_count = width // (col_devices * BLOCK)
    total_rows = rows_dev * col_devices * lax.axis_size("row")
    stretch = math.sqrt(total_rows)
    scaled = jacobian * jnp.sqrt(counts.astype(jnp.float32))[:, None]
    blocks = scaled.reshape(rows_dev, slot_count, col_devices, BLOCK)
    arrived = lax.all_to_all(blocks, "col", split_axis=2, concat_axis=0, tiled=True)
    matrix = arrived.reshape(col_devices * rows_dev, slot_count, BLOCK)
    block_ids = jnp.arange(slot_count, dtype=jnp.int32) * col_devices + lax.axis_index("col")
    couplings = []
    for panel_step in range(PANELS):
        panel_cols = matrix[:, 0, :]
        first_gram = lax.psum(gram_of(panel_cols), "row")
        basis, triangle = complete(panel_cols, first_gram)
        basis = from_root(basis, "col", panel_step)
        products = jnp.einsum(
            "lb,lsc->bsc", basis, matrix, precision=HIGH, preferred_element_type=jnp.float32
        )
        coupling = lax.psum(products, "row")
        before_mask = (block_ids < panel_step)[None, :, None]
        current_mask = (block_ids == panel_step)[None, :, None]
        later_mask = (block_ids > panel_step)[None, :, None]
        coupling = jnp.where(
            before_mask,
            jnp.zeros_like(coupling),
            jnp.where(current_mask, triangle[:, None, :], coupling),
        )
        update = matrix - jnp.einsum(
            "lb,bsc->lsc", basis, coupling, precision=HIGH, preferred_element_type=jnp.float32
        )
        matrix = jnp.where(
            later_mask, update, jnp.where(current_mask, (basis * stretch)[:, None, :], matrix)
        )
        couplings.append(coupling)
    factored = matrix.reshape(col_devices, 1, rows_dev, slot_count, 1, BLOCK)
    r_rows = jnp.concatenate(couplings, 0).reshape(PANELS * BLOCK, slot_count, 1, BLOCK)
    return (factored, r_rows)


def solution(mesh):
    placed = (P(("col", "row"), None), P(("col", "row")))
    return jax.shard_map(
        shards,
        mesh=mesh,
        in_specs=placed,
        out_specs=(P(None, "row", None, None, "col", None), P(None, None, "col", None)),
        check_vma=False,
    )
```

profile of v0, /device:TPU:0, one launch (start us, length us, event | category | flops | bytes accessed | tf_op | source)
XLA Modules:
  0.0 353.6 jit_solution(1345375849089742614)
XLA Ops:
  7.2 0.0 all-reduce.7.cloned.1.call-start
  7.2 0.7 convert_sqrt_fusion
  7.9 1.0 multiply_bitcast_fusion
  8.9 14.4 %all_to_all.15 = f32[32,1,8,128]{3,0,1,2:T(8,128)S(1)} all-to-all(f32[32,1,8,128]{3,0,1,2:T(8,128)S(1)} %copy.30), channel_id=1, replica_groups=mesh['col'=8,'row'=4] {'col'}, dimensions={2} | all-to-all | bytes 262144 | tf_op jit(solution)/shard_map/all_to_all | solution.py:38
  23.3 1.0 convolution_bitcast_fusion.2
  24.3 0.0 all-reduce.7.cloned.1.call-update
  24.4 0.0 all-reduce.9.cloned.1.call-start
  24.4 28.9 %all-reduce.7.cloned.1.call-done = f32[128,128]{0,1:T(8,128)} async-done(((f32[128,128]{0,1:T(8,128)}), f32[128,128]{0,1:T(8,128)}) %all-reduce.7.cloned.1.call-update) | async-done | bytes 65552 | tf_op jit(solution)/shard_map/psum | solution.py:44
  53.4 1.0 copy.32
  54.4 0.0 copy-done.2
  54.4 11.7 %cholesky.44 = f32[128,128]{1,0:T(8,128)S(1)} custom-call(f32[128,128]{1,0:T(8,128)S(1)} %fusion.13), custom_call_target="Cholesky" | custom-call | tf_op jit(solution)/shard_map/jit(cholesky)/cholesky | solution.py:25
  66.2 0.6 compare_reduce_fusion.1
  66.8 0.7 select_bitcast_fusion.1
  67.5 9.8 %custom-call.6 = f32[1,128,128]{1,2,0:T(8,128)S(1)} custom-call(f32[1,128,128]{2,1,0:T(8,128)S(1)} %select_bitcast_fusion.1), custom_call_target="InvertDiagBlocksLowerTriangular" | custom-call | tf_op jit(solution)/shard_map/jit(_solve_triangular)/triangular_solve | solution.py:26
  77.3 1.0 fusion.3
  78.3 0.0 all-reduce.9.cloned.1.call-update
  78.3 0.0 all-reduce.11.cloned.1.call-start
  78.3 69.8 %all-reduce.9.cloned.1.call-done = f32[256,128]{0,1:T(8,128)} async-done(((f32[256,128]{0,1:T(8,128)}), f32[256,128]{0,1:T(8,128)}) %all-reduce.9.cloned.1.call-update) | async-done | bytes 131088 | tf_op jit(solution)/shard_map/psum | solution.py:17
  148.1 1.9 convolution_bitcast_fusion.1
  150.0 0.0 all-reduce.11.cloned.1.call-update
  150.1 0.0 all-reduce.13.cloned.1.call-start
  150.1 0.1 copy.34
  150.2 0.0 copy-start.1
  150.2 31.2 %all-reduce.11.cloned.1.call-done = f32[128,1,128]{0,2,1:T(8,128)} async-done(((f32[128,1,128]{0,2,1:T(8,128)}), f32[128,1,128]{0,2,1:T(8,128)}) %all-reduce.11.cloned.1.call-update) | async-done | bytes 65552 | tf_op jit(solution)/shard_map/psum | solution.py:50
  181.4 0.7 fusion.7
  182.1 0.0 copy-done.1
  182.1 0.3 fusion
  182.3 0.9 fusion.15
  183.3 0.0 all-reduce.13.cloned.1.call-update
  183.3 0.2 all-reduce.15.cloned.1.call-start
  183.5 31.8 %all-reduce.13.cloned.1.call-done = f32[128,128]{0,1:T(8,128)} async-done(((f32[128,128]{0,1:T(8,128)}), f32[128,128]{0,1:T(8,128)}) %all-reduce.13.cloned.1.call-update) | async-done | bytes 65552 | tf_op jit(solution)/shard_map/psum | solution.py:44
  215.3 1.0 copy.38
  216.3 11.7 %cholesky.55 = f32[128,128]{1,0:T(8,128)S(1)} custom-call(f32[128,128]{1,0:T(8,128)S(1)} %fusion.10), custom_call_target="Cholesky" | custom-call | tf_op jit(solution)/shard_map/jit(cholesky)/cholesky | solution.py:25
  228.1 0.6 compare_reduce_fusion
  228.7 0.7 select_bitcast_fusion
  229.4 9.8 %custom-call.7 = f32[1,128,128]{1,2,0:T(8,128)S(1)} custom-call(f32[1,128,128]{2,1,0:T(8,128)S(1)} %select_bitcast_fusion), custom_call_target="InvertDiagBlocksLowerTriangular" | custom-call | tf_op jit(solution)/shard_map/jit(_solve_triangular)/triangular_solve | solution.py:26
  239.2 1.0 fusion.2
  240.2 0.0 all-reduce.15.cloned.1.call-update
  240.2 0.0 all-reduce.17.cloned.1.call-start
  240.3 69.8 %all-reduce.15.cloned.1.call-done = f32[256,128]{0,1:T(8,128)} async-done(((f32[256,128]{0,1:T(8,128)}), f32[256,128]{0,1:T(8,128)}) %all-reduce.15.cloned.1.call-update) | async-done | bytes 131088 | tf_op jit(solution)/shard_map/psum | solution.py:17
  310.1 1.8 convolution_bitcast_fusion
  311.9 0.0 all-reduce.17.cloned.1.call-update
  311.9 31.4 %all-reduce.17.cloned.1.call-done = f32[128,1,128]{0,2,1:T(8,128)} async-done(((f32[128,1,128]{0,2,1:T(8,128)}), f32[128,1,128]{0,2,1:T(8,128)}) %all-reduce.17.cloned.1.call-update) | async-done | bytes 65552 | tf_op jit(solution)/shard_map/psum | solution.py:50
  343.3 1.5 fusion.6
  344.8 0.8 copy.43
  345.6 0.1 copy-done
  345.7 0.3 fusion.1
  346.0 0.8 copy.41
  (11 shorter events, 0.2 us)
Async XLA Ops:
  7.2 46.2 %all-reduce.7.cloned.1.call-start = ((), (), s32[]{:S(2)}) async-start(), calls=%async_computation.1 | async-start | bytes 131072 | tf_op jit(solution)/shard_map/psum | solution.py:44
  24.4 123.7 %all-reduce.9.cloned.1.call-start = ((), (), s32[]{:S(2)}) async-start(), calls=%async_computation.2 | async-start | bytes 262144 | tf_op jit(solution)/shard_map/psum | solution.py:17
  53.4 1.0 copy-start.2
  78.3 103.1 %all-reduce.11.cloned.1.call-start = ((), (), s32[]{:S(2)}) async-start(), calls=%async_computation.3 | async-start | bytes 131072 | tf_op jit(solution)/shard_map/psum | solution.py:50
  150.1 65.3 %all-reduce.13.cloned.1.call-start = ((), (), s32[]{:S(2)}) async-start(), calls=%async_computation.4 | async-start | bytes 131072 | tf_op jit(solution)/shard_map/psum | solution.py:44
  150.2 31.8 %copy-start.1 = (f32[256,128]{0,1:T(8,128)S(1)}, f32[256,128]{0,1:T(8,128)}, u32[]{:S(2)}) copy-start(f32[256,128]{0,1:T(8,128)} %all-reduce.9.cloned.1.call-done) | copy-start | bytes 393220
  183.3 126.8 %all-reduce.15.cloned.1.call-start = ((), (), s32[]{:S(2)}) async-start(), calls=%async_computation.5 | async-start | bytes 262144 | tf_op jit(solution)/shard_map/psum | solution.py:17
  215.3 1.0 copy-start.3
  240.2 103.1 %all-reduce.17.cloned.1.call-start = ((), (), s32[]{:S(2)}) async-start(), calls=%async_computation.6 | async-start | bytes 131072 | tf_op jit(solution)/shard_map/psum | solution.py:50
  344.8 0.9 copy-start
Sparse Core Ops, SparseCore 0:
  24.5 28.8 all-reduce.6
  78.4 69.6 all-reduce.8
  151.0 30.3 all-reduce.10
  184.2 31.0 all-reduce.12
  240.3 69.6 all-reduce.14
  312.9 30.3 all-reduce.16
where the time goes:
time: 354 us
  waiting for transfers between devices  263 us (74%)
  other arithmetic  49.6 us (14%)
  blocking collectives  14.4 us (4%)
  between operations  14.3 us (4%)
  matrix products  8.13 us (2%)
  local copies, waits for them, and re-layouts  3.81 us (1%)
    psum x2, waiting for transfers between devices, from_root(): return lax.psum(kept, axis)  140 us
    psum x2, waiting for transfers between devices, shards(): coupling = lax.psum(products, 'row')  62.5 us
    psum x2, waiting for transfers between devices, shards(): first_gram = lax.psum(gram_of(panel_cols), 'row')  60.8 us
    another operation x6, other arithmetic, complete(): lower_one = jnp.linalg.cholesky(first_gram)  24.8 us
    another operation x4, other arithmetic, complete(): jax.scipy.linalg.solve_triangular(lower_one, panel_cols.T, lower=True)  20.9 us
    all_to_all x1, blocking collectives, shards(): lax.all_to_all(blocks, 'col', split_axis=2, concat_axis=0, tiled=True)  14.4 us
  transfers between devices with their start and end apart: 6, of which 6 were waited for; matrix products, arithmetic and copies ran while one was open for 0% of the time, Pallas kernels for 0%

commit v1 on v0

v1 whole, which is shorter than its diff:
```python
import functools
import math

import jax
import jax.numpy as jnp
from jax import lax
from jax.experimental import pallas as pl
from jax.experimental.pallas import tpu as pltpu
from jax.sharding import PartitionSpec as P

BLOCK = 128
WIDE = 2 * BLOCK
HALF = BLOCK // 2
HIGH = lax.Precision.HIGHEST
MESH = pl.DeviceIdType.MESH
F32 = jnp.float32


def mm(a, b, ca=1, cb=0):
    return lax.dot_general(
        a, b, (((ca,), (cb,)), ((), ())), precision=HIGH, preferred_element_type=F32
    )


def exchange_kernel(
    n_col, chunk, jac, cnt, pan, own, gt, gb,
    sc, part_t, part_b, half_t, half_b, in_t, in_b, out_t, out_b,
    send_p, recv_p, send_a, recv_a, send_r, recv_r,
):
    rows = jac.shape[0]
    c = lax.axis_index("col")
    r = lax.axis_index("row")
    core = lax.rem(r, 2)
    sib = r + 1 - 2 * core
    across = lax.rem(r + 2, 4)

    barrier = pltpu.get_barrier_semaphore()

    def greet(i, carry):
        pl.semaphore_signal(
            barrier, inc=1, device_id=(lax.rem(c + i, n_col), r), device_id_type=MESH
        )
        return carry

    lax.fori_loop(1, n_col, greet, 0)
    for other in (sib, across):
        pl.semaphore_signal(barrier, inc=1, device_id=(c, other), device_id_type=MESH)

    root = jnp.sqrt(cnt[...].astype(F32))
    spread = jnp.broadcast_to(root, (rows, rows))
    eye = lax.broadcasted_iota(jnp.int32, (rows, rows), 0) == lax.broadcasted_iota(
        jnp.int32, (rows, rows), 1
    )
    column = jnp.sum(jnp.where(eye, spread, 0.0), axis=1, keepdims=True)
    sc[...] = jac[...] * column
    mine = pl.ds(pl.multiple_of(c * rows, rows), rows)

    pl.semaphore_wait(barrier, n_col + 1)

    def send_panel(i):
        return pltpu.make_async_remote_copy(
            src_ref=sc.at[:, pl.ds(0, WIDE)],
            dst_ref=pan.at[mine, :],
            send_sem=send_p.at[i],
            recv_sem=recv_p.at[i],
            device_id=(lax.rem(c + i, n_col), r),
            device_id_type=MESH,
        )

    def send_own(i):
        t = lax.rem(c + i, n_col)
        return pltpu.make_async_remote_copy(
            src_ref=sc.at[:, pl.ds(pl.multiple_of(t * BLOCK, BLOCK), BLOCK)],
            dst_ref=own.at[mine, :],
            send_sem=send_a.at[i],
            recv_sem=recv_a.at[i],
            device_id=(t, r),
            device_id_type=MESH,
        )

    def loop(body):
        def step(i, carry):
            body(i)
            return carry

        lax.fori_loop(1, n_col, step, 0)

    loop(lambda i: send_panel(i).start())
    loop(lambda i: send_own(i).start())
    pan[mine, :] = sc[:, :WIDE]
    own[mine, :] = sc[:, pl.ds(pl.multiple_of(c * BLOCK, BLOCK), BLOCK)]
    loop(lambda i: send_panel(i).wait_recv())
    part_t[...] = jnp.zeros_like(part_t)
    part_b[...] = jnp.zeros_like(part_b)

    def gram_panel(k, carry):
        at = pl.ds(pl.multiple_of(k * chunk, chunk), chunk)
        p0, p1 = pan[at, :BLOCK], pan[at, BLOCK:]
        part_t[:, :BLOCK] += mm(p0, p0, 0, 0)
        part_t[:, BLOCK:WIDE] += mm(p0, p1, 0, 0)
        part_b[:, :BLOCK] += mm(p1, p1, 0, 0)
        return carry

    lax.fori_loop(0, n_col * rows // chunk, gram_panel, 0)
    loop(lambda i: send_own(i).wait_recv())

    def gram_own(k, carry):
        at = pl.ds(pl.multiple_of(k * chunk, chunk), chunk)
        a = own[at, :]
        part_t[:, WIDE:] += mm(pan[at, :BLOCK], a, 0, 0)
        part_b[:, BLOCK:] += mm(pan[at, BLOCK:], a, 0, 0)
        return carry

    lax.fori_loop(0, n_col * rows // chunk, gram_own, 0)

    here = pl.ds(pl.multiple_of(core * HALF, HALF), HALF)
    there = pl.ds(pl.multiple_of((1 - core) * HALF, HALF), HALF)

    def swap(src, dst, slot, other):
        return pltpu.make_async_remote_copy(
            src_ref=src,
            dst_ref=dst,
            send_sem=send_r.at[slot],
            recv_sem=recv_r.at[slot],
            device_id=(c, other),
            device_id_type=MESH,
        )

    first = [
        swap(part_t.at[there, :], in_t, 0, sib),
        swap(part_b.at[there, :], in_b, 1, sib),
    ]
    for copy in first:
        copy.start()
    first[0].wait_recv()
    half_t[...] = part_t[here, :] + in_t[...]
    second = [swap(half_t, out_t, 2, across), swap(half_b, out_b, 3, across)]
    second[0].start()
    first[1].wait_recv()
    half_b[...] = part_b[here, :] + in_b[...]
    second[1].start()
    second[0].wait_recv()
    gt[here, :] = half_t[...] + out_t[...]
    third = [
        swap(gt.at[here, :], gt.at[here, :], 4, sib),
        swap(gb.at[here, :], gb.at[here, :], 5, sib),
    ]
    third[0].start()
    second[1].wait_recv()
    gb[here, :] = half_b[...] + out_b[...]
    third[1].start()
    for copy in third:
        copy.wait_recv()
    for copy in first + second + third:
        copy.wait_send()
    loop(lambda i: send_panel(i).wait_send())
    loop(lambda i: send_own(i).wait_send())


def eliminate(m):
    row = lax.broadcasted_iota(jnp.int32, (8, BLOCK), 0)
    for kb in range(BLOCK // 8):
        r0 = 8 * kb
        left = m[r0 : r0 + 8, :BLOCK]
        right = m[r0 : r0 + 8, BLOCK:]
        cols = [jnp.broadcast_to(left[:, r0 + k : r0 + k + 1], (8, BLOCK)) for k in range(8)]
        diag = jnp.zeros((8, BLOCK), F32)
        for k in range(8):
            pivot = jnp.broadcast_to(cols[k][k : k + 1, :], (8, BLOCK))
            diag = jnp.where(row == k, pivot, diag)
            if k < 7:
                factor = jnp.where(row > k, cols[k] / pivot, 0.0)
                for j in range(k + 1, 8):
                    cols[j] = cols[j] - factor * cols[j][k : k + 1, :]
                left = left - factor * left[k : k + 1, :]
                right = right - factor * right[k : k + 1, :]
        scale = lax.rsqrt(diag)
        left = left * scale
        right = right * scale
        m[r0 : r0 + 8, :BLOCK] = left
        m[r0 : r0 + 8, BLOCK:] = right
        if kb < BLOCK // 8 - 1:
            after = mm(left, jnp.concatenate([left, right], axis=1), 0, 0)
            m[r0 + 8 :, :] -= after[r0 + 8 :, :]


def finish_kernel(n_col, stretch, chunk, pan, own, gt, gb, fac, rr, m):
    c = lax.axis_index("col")
    at_row = lax.broadcasted_iota(jnp.int32, (BLOCK, BLOCK), 0)
    at_col = lax.broadcasted_iota(jnp.int32, (BLOCK, BLOCK), 1)
    eye = jnp.where(at_row == at_col, 1.0, 0.0).astype(F32)
    upper = at_row <= at_col
    m[:, :BLOCK] = gt[:, :BLOCK]
    m[:, BLOCK:] = eye
    eliminate(m)
    w0 = m[:, BLOCK:]
    r00 = jnp.where(upper, m[:, :BLOCK], 0.0)
    r01 = mm(w0, gt[:, BLOCK:WIDE])
    r0j = mm(w0, gt[:, WIDE:])
    m[:, :BLOCK] = gb[:, :BLOCK] - mm(r01, r01, 0, 0)
    m[:, BLOCK:] = eye
    eliminate(m)
    w1 = m[:, BLOCK:]
    r11 = jnp.where(upper, m[:, :BLOCK], 0.0)
    r1j = mm(w1, gb[:, BLOCK:] - mm(r01, r0j, 0, 0))
    zero, one = c == 0, c == 1
    rr[:BLOCK, :] = jnp.where(zero, r00, jnp.where(one, r01, r0j))
    rr[BLOCK:, :] = jnp.where(zero, 0.0, jnp.where(one, r11, r1j))

    def tail(k, carry):
        at = pl.ds(pl.multiple_of(k * chunk, chunk), chunk)
        q0 = mm(pan[at, :BLOCK], w0, 1, 1)
        q1 = mm(pan[at, BLOCK:] - mm(q0, r01), w1, 1, 1)
        later = own[at, :] - mm(q0, r0j) - mm(q1, r1j)
        fac[at, :] = jnp.where(zero, q0 * stretch, jnp.where(one, q1 * stretch, later))
        return carry

    lax.fori_loop(0, pan.shape[0] // chunk, tail, 0)


def shards(n_col, n_row, jacobian, counts):
    rows_dev, width = jacobian.shape
    assert width == n_col * BLOCK and n_row == 4
    local = n_col * rows_dev
    chunk = min(256, local)
    stretch = math.sqrt(local * n_row)
    vmem = pl.BlockSpec(memory_space=pltpu.VMEM)
    shape = lambda *dims: jax.ShapeDtypeStruct(dims, F32)
    limit = 48 * 1024 * 1024
    pan, own, gt, gb = pl.pallas_call(
        functools.partial(exchange_kernel, n_col, chunk),
        out_shape=(
            shape(local, WIDE), shape(local, BLOCK), shape(BLOCK, 3 * BLOCK), shape(BLOCK, WIDE),
        ),
        in_specs=[vmem] * 2,
        out_specs=(vmem,) * 4,
        scratch_shapes=[
            pltpu.VMEM((rows_dev, width), F32),
            pltpu.VMEM((BLOCK, 3 * BLOCK), F32),
            pltpu.VMEM((BLOCK, WIDE), F32),
            pltpu.VMEM((HALF, 3 * BLOCK), F32),
            pltpu.VMEM((HALF, WIDE), F32),
            pltpu.VMEM((HALF, 3 * BLOCK), F32),
            pltpu.VMEM((HALF, WIDE), F32),
            pltpu.VMEM((HALF, 3 * BLOCK), F32),
            pltpu.VMEM((HALF, WIDE), F32),
            pltpu.SemaphoreType.DMA((n_col,)),
            pltpu.SemaphoreType.DMA((n_col,)),
            pltpu.SemaphoreType.DMA((n_col,)),
            pltpu.SemaphoreType.DMA((n_col,)),
            pltpu.SemaphoreType.DMA((6,)),
            pltpu.SemaphoreType.DMA((6,)),
        ],
        compiler_params=pltpu.CompilerParams(
            collective_id=0, has_side_effects=True, vmem_limit_bytes=limit
        ),
    )(jacobian, counts.reshape(1, rows_dev))
    fac, rr = pl.pallas_call(
        functools.partial(finish_kernel, n_col, stretch, chunk),
        out_shape=(shape(local, BLOCK), shape(WIDE, BLOCK)),
        in_specs=[vmem] * 4,
        out_specs=(vmem,) * 2,
        scratch_shapes=[pltpu.VMEM((BLOCK, WIDE), F32)],
        compiler_params=pltpu.CompilerParams(vmem_limit_bytes=limit),
    )(pan, own, gt, gb)
    factored = fac.reshape(n_col, 1, rows_dev, 1, 1, BLOCK)
    return (factored, rr.reshape(WIDE, 1, 1, BLOCK))


def solution(mesh):
    placed = (P(("col", "row"), None), P(("col", "row")))
    return jax.shard_map(
        functools.partial(shards, mesh.shape["col"], mesh.shape["row"]),
        mesh=mesh,
        in_specs=placed,
        out_specs=(P(None, "row", None, None, "col", None), P(None, None, "col", None)),
        check_vma=False,
    )
```

time: 354 us -> 44.7 us (0.13)
  waiting for transfers between devices: 263 us -> 0 us
  other arithmetic: 49.6 us -> 0 us
  Pallas kernels: 0 us -> 42.4 us
  blocking collectives: 14.4 us -> 0 us
  between operations: 14.3 us -> 0.65 us
  matrix products: 8.13 us -> 0 us
    psum x6 -> x0, waiting for transfers between devices: 263 us -> none  [the longest x2 140 us: from_root(): return lax.psum(kept, axis)]
    another operation x10 -> x0, other arithmetic: 45.7 us -> none  [the longest x6 24.8 us: complete(): lower_one = jnp.linalg.cholesky(first_gram)]
    pallas_call x0 -> x2, Pallas kernels: none -> 42.4 us  [the longest x1 23.2 us: shards(): pl.pallas_call(functools.partial(exchange_kernel, n_col, chunk), out_shap...]
    all_to_all x1 -> x0, blocking collectives: 14.4 us -> none  [shards(): lax.all_to_all(blocks, 'col', split_axis=2, concat_axis=0, tiled=True)]
    dot_general x6 -> x0, matrix products: 6.19 us -> none  [the longest x2 3.73 us: shards(): jnp.einsum('lb,lsc->bsc', basis, matrix, precision=HIGH, preferred_elemen...]
  transfers between devices with their start and end apart: 6 -> 0, of which waited for: 6 -> 0; matrix products, arithmetic and copies ran while one was open for 0% -> 0% of each run, Pallas kernels for 0% -> 0%
where the time goes in v1:
time: 44.7 us; the launch traced here: 44.6 us
  Pallas kernels  42.4 us (95%)
  local copies, waits for them, and re-layouts  1.55 us (3%)
  between operations  0.65 us (1%)
    pallas_call x1, Pallas kernels, shards(): pl.pallas_call(functools.partial(exchange_kernel, n_col, chunk), out_shap...  23.2 us
    pallas_call x1, Pallas kernels, shards(): pl.pallas_call(functools.partial(finish_kernel, n_col, stretch, chunk), o...  19.2 us
    unnamed x4, local copies, waits for them, and re-layouts  1.55 us

profile of v1, /device:TPU:0, one launch (start us, length us, event | category | flops | bytes accessed | tf_op | source)
XLA Modules:
  0.0 44.6 jit_solution(9629078069649618271)
XLA Ops:
  0.6 0.0 copy-start.1
  0.6 0.6 %copy-done.1 = s32[32]{0:T(128)S(1)} copy-done((s32[32]{0:T(128)S(1)}, s32[32]{0:T(128)}, u32[]{:S(2)}) %copy-start.1) | copy-done | bytes 152
  1.3 0.0 copy-start
  1.3 0.9 %copy-done = f32[32,1024]{1,0:T(8,128)S(1)} copy-done((f32[32,1024]{1,0:T(8,128)S(1)}, f32[32,1024]{1,0:T(8,128)}, u32[]{:S(2)}) %copy-start) | copy-done | bytes 131096
  2.2 23.2 %shard_map.41 = (f32[256,256]{1,0:T(8,128)S(1)}, f32[256,128]{1,0:T(8,128)S(1)}, f32[128,384]{1,0:T(8,128)S(1)}, f32[128,256]{1,0:T(8,128)S(1)}) custom-call(f32[32,1024]{1,0:T(8,128)S(1)} %copy-done, s32[1,32]{1,0:T(1,128)S(1)} %bitcast.7), custom_call_target="tpu_custom_call" | custom-call | tf_op jit(solution)/shard_map/pallas_call | solution.py:230
  25.4 19.2 %shard_map.42 = (f32[256,128]{1,0:T(8,128)}, f32[256,128]{1,0:T(8,128)}) custom-call(f32[256,256]{1,0:T(8,128)S(1)} %get-tuple-element.8.pan, f32[256,128]{1,0:T(8,128)S(1)} %get-tuple-element.9.own, f32[128,384]{1,0:T(8,128)S(1)} %get-tuple-element.10.gt, f32[128,256]{1,0:T(8,128)S(1)} %get-tuple-element.11.gb), custom_call_target="tpu_custom_call" | custom-call | tf_op jit(solution)/shard_map/pallas_call | solution.py:258
Async XLA Ops:
  0.6 0.7 %copy-start.1 = (s32[32]{0:T(128)S(1)}, s32[32]{0:T(128)}, u32[]{:S(2)}) copy-start(s32[32]{0:T(128)} %param.3) | copy-start | bytes 388
  1.3 0.9 %copy-start = (f32[32,1024]{1,0:T(8,128)S(1)}, f32[32,1024]{1,0:T(8,128)}, u32[]{:S(2)}) copy-start(f32[32,1024]{1,0:T(8,128)} %jac.1) | copy-start | bytes 393220

commit v2 on v0

v2 whole, which is shorter than its diff:
```python
import functools
import math

import jax
import jax.numpy as jnp
from jax import lax
from jax.experimental import pallas as pl
from jax.experimental.pallas import tpu as pltpu
from jax.sharding import PartitionSpec as P

BLOCK = 128
WIDE = 2 * BLOCK
HALF = BLOCK // 2
STEP = 16
B16 = jnp.bfloat16
HIGH = lax.Precision.HIGHEST
MESH = pl.DeviceIdType.MESH
F32 = jnp.float32


def mm(a, b, ca=1, cb=0):
    return lax.dot_general(
        a, b, (((ca,), (cb,)), ((), ())), precision=HIGH, preferred_element_type=F32
    )


def split3(x):
    high = x.astype(B16)
    x = x - high.astype(F32)
    mid = x.astype(B16)
    return high, mid, (x - mid.astype(F32)).astype(B16)


def outer(rows):
    h, m, l = split3(rows)
    lh, lm, ll = h[:, :BLOCK], m[:, :BLOCK], l[:, :BLOCK]
    a = jnp.concatenate([lh, lh, lm, lh, ll, lm], axis=0)
    b = jnp.concatenate([h, m, h, l, h, m], axis=0)
    return lax.dot_general(a, b, (((0,), (0,)), ((), ())), preferred_element_type=F32)


def recip(x):
    guess = pl.reciprocal(x, approx=True)
    return guess * (2.0 - x * guess)


def eliminate(m, hooks):
    row = lax.broadcasted_iota(jnp.int32, (STEP, BLOCK), 0)
    for kb in range(BLOCK // STEP):
        r0 = STEP * kb
        left = m[r0 : r0 + STEP, :BLOCK]
        right = m[r0 : r0 + STEP, BLOCK:]
        cols = [
            jnp.broadcast_to(left[:, r0 + k : r0 + k + 1], (STEP, BLOCK)) for k in range(STEP)
        ]
        diag = jnp.zeros((STEP, BLOCK), F32)
        for k in range(0, STEP, 2):
            c1, c2 = cols[k], cols[k + 1]
            a, b, e = c1[k : k + 1, :], c1[k + 1 : k + 2, :], c2[k + 1 : k + 2, :]
            g = b * recip(a)
            diag = jnp.where(row == k, a, jnp.where(row == k + 1, e - b * g, diag))
            l1, l2 = left[k : k + 1, :], left[k + 1 : k + 2, :]
            q1, q2 = right[k : k + 1, :], right[k + 1 : k + 2, :]
            f1 = jnp.where(row == k + 1, g, 0.0)
            if k < STEP - 2:
                inv = recip(a * e - b * b)
                below = row > k + 1
                f2 = jnp.where(below, (a * c2 - b * c1) * inv, 0.0)
                f1 = jnp.where(below, (e * c1 - b * c2) * inv, f1)
                for j in range(k + 2, STEP):
                    cols[j] = cols[j] - f1 * cols[j][k : k + 1, :] - f2 * cols[j][k + 1 : k + 2, :]
                left = left - f2 * l2
                right = right - f2 * q2
            left = left - f1 * l1
            right = right - f1 * q1
        scale = lax.rsqrt(diag)
        left = left * scale
        right = right * scale
        m[r0 : r0 + STEP, :BLOCK] = left
        m[r0 : r0 + STEP, BLOCK:] = right
        if kb < BLOCK // STEP - 1:
            after = outer(jnp.concatenate([left, right], axis=1))
            m[r0 + STEP :, :] -= after[r0 + STEP :, :]
        if kb in hooks:
            hooks[kb]()


def kernel(
    n_col, stretch, chunk, jac_any, cnt_any, fac, rr,
    jac, cnt, sc, pan0, pan1, own, g0, in0, out0,
    part1, in1, half1, out1, g1, part2, in2, half2, out2, g2, m, r0j, u1j,
    load, send_p0, recv_p0, send_p1, recv_p1, send_a, recv_a, send_r, recv_r,
):
    rows = jac.shape[0]
    local = pan0.shape[0]
    c = lax.axis_index("col")
    r = lax.axis_index("row")
    core = lax.rem(r, 2)
    sib = r + 1 - 2 * core
    across = lax.rem(r + 2, 4)
    slant = sib + 2 - 4 * (sib // 2)

    loads = [
        pltpu.make_async_copy(jac_any, jac, load.at[0]),
        pltpu.make_async_copy(cnt_any, cnt, load.at[1]),
    ]
    for copy in loads:
        copy.start()
    barrier = pltpu.get_barrier_semaphore()

    def loop(body):
        def step(i, carry):
            body(i)
            return carry

        lax.fori_loop(1, n_col, step, 0)

    loop(
        lambda i: pl.semaphore_signal(
            barrier, inc=1, device_id=(lax.rem(c + i, n_col), r), device_id_type=MESH
        )
    )
    for other in (sib, across, slant):
        pl.semaphore_signal(barrier, inc=1, device_id=(c, other), device_id_type=MESH)
    for copy in loads:
        copy.wait()

    root = jnp.sqrt(cnt[...].astype(F32))
    spread = jnp.broadcast_to(root, (rows, rows))
    eye_rows = lax.broadcasted_iota(jnp.int32, (rows, rows), 0) == lax.broadcasted_iota(
        jnp.int32, (rows, rows), 1
    )
    column = jnp.sum(jnp.where(eye_rows, spread, 0.0), axis=1, keepdims=True)
    sc[...] = jac[...] * column
    mine = pl.ds(pl.multiple_of(c * rows, rows), rows)

    pl.semaphore_wait(barrier, n_col + 2)

    def sender(dst, send, recv, lanes_of):
        def make(i):
            t = lax.rem(c + i, n_col)
            return pltpu.make_async_remote_copy(
                src_ref=sc.at[:, lanes_of(t)],
                dst_ref=dst.at[mine, :],
                send_sem=send.at[i],
                recv_sem=recv.at[i],
                device_id=(t, r),
                device_id_type=MESH,
            )

        return make

    block_of = lambda t: pl.ds(pl.multiple_of(t * BLOCK, BLOCK), BLOCK)
    send_first = sender(pan0, send_p0, recv_p0, lambda t: pl.ds(0, BLOCK))
    send_second = sender(pan1, send_p1, recv_p1, lambda t: pl.ds(BLOCK, BLOCK))
    send_own = sender(own, send_a, recv_a, block_of)
    loop(lambda i: send_first(i).start())
    loop(lambda i: send_second(i).start())
    loop(lambda i: send_own(i).start())
    pan0[mine, :] = sc[:, :BLOCK]
    pan1[mine, :] = sc[:, BLOCK:WIDE]
    own[mine, :] = sc[:, block_of(c)]

    def gram(out, lanes, x, y):
        if local == chunk:
            out[:, lanes] = mm(x[...], y[...], 0, 0)
            return
        out[:, lanes] = jnp.zeros((BLOCK, BLOCK), F32)

        def add(k, carry):
            at = pl.ds(pl.multiple_of(k * chunk, chunk), chunk)
            out[:, lanes] += mm(x[at, :], y[at, :], 0, 0)
            return carry

        lax.fori_loop(0, local // chunk, add, 0)

    def tiles(body):
        def step(k, carry):
            body(pl.ds(pl.multiple_of(k * chunk, chunk), chunk))
            return carry

        if local == chunk:
            body(pl.ds(0, chunk))
        else:
            lax.fori_loop(0, local // chunk, step, 0)

    first, second = slice(0, BLOCK), slice(BLOCK, WIDE)
    here = pl.ds(pl.multiple_of(core * HALF, HALF), HALF)
    there = pl.ds(pl.multiple_of((1 - core) * HALF, HALF), HALF)
    started = []

    def swap(src, dst, slot, other):
        copy = pltpu.make_async_remote_copy(
            src_ref=src,
            dst_ref=dst,
            send_sem=send_r.at[slot],
            recv_sem=recv_r.at[slot],
            device_id=(c, other),
            device_id_type=MESH,
        )
        copy.start()
        started.append(copy)
        return copy

    loop(lambda i: send_first(i).wait_recv())
    gram(g0, first, pan0, pan0)
    pair = swap(g0, in0, 0, sib)
    pair.wait()
    started.remove(pair)
    g0[...] += in0[...]
    straight = swap(g0.at[here, :], out0.at[here, :], 1, across)
    slanted = swap(g0.at[here, :], out0.at[here, :], 2, slant)

    box = {}

    def reduce_a(key, part, into, slot):
        box[key] = swap(part.at[there, :], into, slot, sib)

    def reduce_b(key, part, into, half, out, slot):
        box[key].wait_recv()
        half[...] = part[here, :] + into[...]
        box[key] = swap(half, out, slot, across)

    def reduce_c(key, half, out, total, slot):
        box[key].wait_recv()
        total[here, :] = half[...] + out[...]
        box[key] = swap(total.at[here, :], total.at[here, :], slot, sib)

    loop(lambda i: send_second(i).wait_recv())
    gram(part1, first, pan0, pan1)
    gram(part1, second, pan1, pan1)
    reduce_a(1, part1, in1, 3)
    straight.wait_recv()
    slanted.wait_recv()

    at_row = lax.broadcasted_iota(jnp.int32, (BLOCK, BLOCK), 0)
    at_col = lax.broadcasted_iota(jnp.int32, (BLOCK, BLOCK), 1)
    eye = jnp.where(at_row == at_col, 1.0, 0.0).astype(F32)
    upper = at_row <= at_col
    m[:, :BLOCK] = g0[...] + out0[...]
    m[:, BLOCK:] = eye

    def own_gram():
        loop(lambda i: send_own(i).wait_recv())
        gram(part2, first, pan0, own)
        gram(part2, second, pan1, own)
        reduce_a(2, part2, in2, 4)

    eliminate(
        m,
        {
            0: lambda: reduce_b(1, part1, in1, half1, out1, 5),
            2: own_gram,
            4: lambda: reduce_c(1, half1, out1, g1, 6),
            5: lambda: reduce_b(2, part2, in2, half2, out2, 7),
        },
    )
    w0 = m[:, BLOCK:]
    r00 = jnp.where(upper, m[:, :BLOCK], 0.0)
    box[1].wait_recv()
    r01 = mm(w0, g1[:, :BLOCK])
    m[:, :BLOCK] = g1[:, BLOCK:] - mm(r01, r01, 0, 0)
    m[:, BLOCK:] = eye
    zero, one = c == 0, c == 1

    def basis():
        def tile(at):
            q0 = mm(pan0[at, :], w0, 1, 1)
            pan0[at, :] = q0
            pan1[at, :] = pan1[at, :] - mm(q0, r01)

        tiles(tile)

    def coupling():
        box[2].wait_recv()
        r0j[...] = mm(w0, g2[:, :BLOCK])
        u1j[...] = g2[:, BLOCK:] - mm(r01, r0j[...], 0, 0)
        rr[:BLOCK, :] = jnp.where(zero, r00, jnp.where(one, r01, r0j[...]))

    def update():
        def tile(at):
            own[at, :] = own[at, :] - mm(pan0[at, :], r0j[...])

        tiles(tile)

    eliminate(
        m,
        {
            0: lambda: reduce_c(2, half2, out2, g2, 8),
            1: basis,
            3: coupling,
            4: update,
        },
    )
    w1 = m[:, BLOCK:]
    r11 = jnp.where(upper, m[:, :BLOCK], 0.0)
    r1j = mm(w1, u1j[...])
    rr[BLOCK:, :] = jnp.where(zero, 0.0, jnp.where(one, r11, r1j))

    def tail(at):
        q1 = mm(pan1[at, :], w1, 1, 1)
        later = own[at, :] - mm(q1, r1j)
        fac[at, :] = jnp.where(
            zero, pan0[at, :] * stretch, jnp.where(one, q1 * stretch, later)
        )

    tiles(tail)
    for copy in started:
        copy.wait_send()
    loop(lambda i: send_first(i).wait_send())
    loop(lambda i: send_second(i).wait_send())
    loop(lambda i: send_own(i).wait_send())


def shards(n_col, n_row, jacobian, counts):
    rows_dev, width = jacobian.shape
    assert width == n_col * BLOCK and n_row == 4
    local = n_col * rows_dev
    chunk = min(256, local)
    stretch = math.sqrt(local * n_row)
    vmem = pl.BlockSpec(memory_space=pltpu.VMEM)
    anywhere = pl.BlockSpec(memory_space=pl.ANY)
    shape = lambda *dims: jax.ShapeDtypeStruct(dims, F32)
    buf = lambda *dims: pltpu.VMEM(dims, F32)
    sems = pltpu.SemaphoreType.DMA((n_col,))
    staged = [
        buf(BLOCK, WIDE), buf(HALF, WIDE), buf(HALF, WIDE), buf(HALF, WIDE), buf(BLOCK, WIDE),
    ]
    fac, rr = pl.pallas_call(
        functools.partial(kernel, n_col, stretch, chunk),
        out_shape=(shape(local, BLOCK), shape(WIDE, BLOCK)),
        in_specs=[anywhere] * 2,
        out_specs=(vmem,) * 2,
        scratch_shapes=[
            buf(rows_dev, width), pltpu.VMEM((1, rows_dev), jnp.int32), buf(rows_dev, width),
            buf(local, BLOCK), buf(local, BLOCK), buf(local, BLOCK),
            buf(BLOCK, BLOCK), buf(BLOCK, BLOCK), buf(BLOCK, BLOCK),
            *staged, *staged, buf(BLOCK, WIDE), buf(BLOCK, BLOCK), buf(BLOCK, BLOCK),
            pltpu.SemaphoreType.DMA((2,)), sems, sems, sems, sems, sems, sems,
            pltpu.SemaphoreType.DMA((9,)), pltpu.SemaphoreType.DMA((9,)),
        ],
        compiler_params=pltpu.CompilerParams(
            collective_id=0, has_side_effects=True, vmem_limit_bytes=56 * 1024 * 1024
        ),
    )(jacobian, counts.reshape(1, rows_dev))
    factored = fac.reshape(n_col, 1, rows_dev, 1, 1, BLOCK)
    return (factored, rr.reshape(WIDE, 1, 1, BLOCK))


def solution(mesh):
    placed = (P(("col", "row"), None), P(("col", "row")))
    return jax.shard_map(
        functools.partial(shards, mesh.shape["col"], mesh.shape["row"]),
        mesh=mesh,
        in_specs=placed,
        out_specs=(P(None, "row", None, None, "col", None), P(None, None, "col", None)),
        check_vma=False,
    )
```

time: 354 us -> 31.5 us (0.09)
  waiting for transfers between devices: 263 us -> 0 us
  other arithmetic: 49.6 us -> 0 us
  Pallas kernels: 0 us -> 28.4 us
  blocking collectives: 14.4 us -> 0 us
  between operations: 14.3 us -> 0.65 us
  matrix products: 8.13 us -> 0 us
    psum x6 -> x0, waiting for transfers between devices: 263 us -> none  [the longest x2 140 us: from_root(): return lax.psum(kept, axis)]
    another operation x10 -> x0, other arithmetic: 45.7 us -> none  [the longest x6 24.8 us: complete(): lower_one = jnp.linalg.cholesky(first_gram)]
    pallas_call x0 -> x1, Pallas kernels: none -> 28.4 us  [shards(): pl.pallas_call(functools.partial(kernel, n_col, stretch, chunk), out_shap...]
    all_to_all x1 -> x0, blocking collectives: 14.4 us -> none  [shards(): lax.all_to_all(blocks, 'col', split_axis=2, concat_axis=0, tiled=True)]
    dot_general x6 -> x0, matrix products: 6.19 us -> none  [the longest x2 3.73 us: shards(): jnp.einsum('lb,lsc->bsc', basis, matrix, precision=HIGH, preferred_elemen...]
  transfers between devices with their start and end apart: 6 -> 0, of which waited for: 6 -> 0; matrix products, arithmetic and copies ran while one was open for 0% -> 0% of each run, Pallas kernels for 0% -> 0%
where the time goes in v2:
time: 31.5 us; the launch traced here: 31.3 us
  Pallas kernels  28.4 us (90%)
  local copies, waits for them, and re-layouts  2.26 us (7%)
  between operations  0.65 us (2%)
    pallas_call x1, Pallas kernels, shards(): pl.pallas_call(functools.partial(kernel, n_col, stretch, chunk), out_shap...  28.4 us
    unnamed x4, local copies, waits for them, and re-layouts  2.26 us

profile of v2, /device:TPU:0, one launch (start us, length us, event | category | flops | bytes accessed | tf_op | source)
XLA Modules:
  0.0 31.3 jit_solution(9175989846410786023)
XLA Ops:
  0.6 28.4 %shard_map.41 = (f32[256,128]{1,0:T(8,128)}, f32[256,128]{1,0:T(8,128)}) custom-call(f32[32,1024]{1,0:T(8,128)} %jac_any.1, s32[1,32]{1,0:T(1,128)} %bitcast.9), custom_call_target="tpu_custom_call" | custom-call | tf_op jit(solution)/shard_map/pallas_call | solution.py:329
  29.1 0.0 copy-start
  29.1 1.6 %copy.8 = f32[8,1,32,1,1,128]{5,4,3,2,1,0:T(1,128)} copy(f32[8,1,32,1,1,128]{5,4,3,2,1,0:T(1,128)} %bitcast.8) | data formatting | bytes 262144
  30.7 0.0 copy-done
  30.7 0.7 %copy.9 = f32[256,1,1,128]{3,2,1,0:T(1,128)} copy(f32[256,1,1,128]{3,2,1,0:T(1,128)S(1)} %bitcast.7) | data formatting | bytes 262144
Async XLA Ops:
  29.1 1.6 %copy-start = (f32[256,128]{1,0:T(8,128)S(1)}, f32[256,128]{1,0:T(8,128)}, u32[]{:S(2)}) copy-start(f32[256,128]{1,0:T(8,128)} %get-tuple-element.5) | copy-start | bytes 393220

commit v3 on v2

--- a/solution.py
+++ b/solution.py
@@ -11,6 +11,7 @@
 BLOCK = 128
 WIDE = 2 * BLOCK
 HALF = BLOCK // 2
+PACK = HALF + HALF // 2
 STEP = 16
 B16 = jnp.bfloat16
 HIGH = lax.Precision.HIGHEST
@@ -86,10 +87,10 @@
 
 
 def kernel(
-    n_col, stretch, chunk, jac_any, cnt_any, fac, rr,
-    jac, cnt, sc, pan0, pan1, own, g0, in0, out0,
+    n_col, stretch, chunk, jac_any, cnt_any, x1_out, x2_out, top_out, m_out, u_out,
+    jac, cnt, sc, pan0, pan1, own, g0, pack, in0, out0, top,
     part1, in1, half1, out1, g1, part2, in2, half2, out2, g2, m, r0j, u1j,
-    load, send_p0, recv_p0, send_p1, recv_p1, send_a, recv_a, send_r, recv_r,
+    load, store, send_p0, recv_p0, send_p1, recv_p1, send_a, recv_a, send_r, recv_r,
 ):
     rows = jac.shape[0]
     local = pan0.shape[0]
@@ -155,8 +156,6 @@
     send_second = sender(pan1, send_p1, recv_p1, lambda t: pl.ds(BLOCK, BLOCK))
     send_own = sender(own, send_a, recv_a, block_of)
     loop(lambda i: send_first(i).start())
-    loop(lambda i: send_second(i).start())
-    loop(lambda i: send_own(i).start())
     pan0[mine, :] = sc[:, :BLOCK]
     pan1[mine, :] = sc[:, BLOCK:WIDE]
     own[mine, :] = sc[:, block_of(c)]
@@ -203,13 +202,18 @@
         return copy
 
     loop(lambda i: send_first(i).wait_recv())
+    loop(lambda i: send_second(i).start())
     gram(g0, first, pan0, pan0)
-    pair = swap(g0, in0, 0, sib)
+    low_lane = lax.broadcasted_iota(jnp.int32, (PACK - HALF, BLOCK), 1) < HALF
+    pack[:HALF, :] = g0[:HALF, :]
+    pack[HALF:, :] = jnp.where(low_lane, pltpu.roll(g0[PACK:, :], HALF, 1), g0[HALF:PACK, :])
+    pair = swap(pack, in0, 0, sib)
     pair.wait()
     started.remove(pair)
-    g0[...] += in0[...]
-    straight = swap(g0.at[here, :], out0.at[here, :], 1, across)
-    slanted = swap(g0.at[here, :], out0.at[here, :], 2, slant)
+    pack[...] += in0[...]
+    part = pl.ds(pl.multiple_of(core * (PACK // 2), PACK // 2), PACK // 2)
+    straight = swap(pack.at[part, :], out0.at[part, :], 1, across)
+    slanted = swap(pack.at[part, :], out0.at[part, :], 2, slant)
 
     box = {}
 
@@ -229,6 +233,7 @@
     loop(lambda i: send_second(i).wait_recv())
     gram(part1, first, pan0, pan1)
     gram(part1, second, pan1, pan1)
+    loop(lambda i: send_own(i).start())
     reduce_a(1, part1, in1, 3)
     straight.wait_recv()
     slanted.wait_recv()
@@ -237,7 +242,10 @@
     at_col = lax.broadcasted_iota(jnp.int32, (BLOCK, BLOCK), 1)
     eye = jnp.where(at_row == at_col, 1.0, 0.0).astype(F32)
     upper = at_row <= at_col
-    m[:, :BLOCK] = g0[...] + out0[...]
+    low = pack[HALF:, :] + out0[HALF:, :]
+    m[:HALF, :BLOCK] = pack[:HALF, :] + out0[:HALF, :]
+    m[HALF:PACK, :BLOCK] = low
+    m[PACK:, :BLOCK] = pltpu.roll(low, HALF, 1)
     m[:, BLOCK:] = eye
 
     def own_gram():
@@ -250,9 +258,8 @@
         m,
         {
             0: lambda: reduce_b(1, part1, in1, half1, out1, 5),
-            2: own_gram,
             4: lambda: reduce_c(1, half1, out1, g1, 6),
-            5: lambda: reduce_b(2, part2, in2, half2, out2, 7),
+            5: own_gram,
         },
     )
     w0 = m[:, BLOCK:]
@@ -263,6 +270,13 @@
     m[:, BLOCK:] = eye
     zero, one = c == 0, c == 1
 
+    saved = []
+
+    def save(src, dst, slot):
+        copy = pltpu.make_async_copy(src, dst, store.at[slot])
+        copy.start()
+        saved.append(copy)
+
     def basis():
         def tile(at):
             q0 = mm(pan0[at, :], w0, 1, 1)
@@ -270,46 +284,75 @@
             pan1[at, :] = pan1[at, :] - mm(q0, r01)
 
         tiles(tile)
+        save(pan1, x1_out, 0)
 
     def coupling():
         box[2].wait_recv()
         r0j[...] = mm(w0, g2[:, :BLOCK])
         u1j[...] = g2[:, BLOCK:] - mm(r01, r0j[...], 0, 0)
-        rr[:BLOCK, :] = jnp.where(zero, r00, jnp.where(one, r01, r0j[...]))
+        top[...] = jnp.where(zero, r00, jnp.where(one, r01, r0j[...]))
+        save(top, top_out, 1)
+        save(u1j, u_out, 2)
 
     def update():
         def tile(at):
-            own[at, :] = own[at, :] - mm(pan0[at, :], r0j[...])
+            q0 = pan0[at, :]
+            own[at, :] = jnp.where(zero, q0 * stretch, own[at, :] - mm(q0, r0j[...]))
 
         tiles(tile)
+        save(own, x2_out, 3)
 
     eliminate(
         m,
         {
-            0: lambda: reduce_c(2, half2, out2, g2, 8),
+            0: lambda: reduce_b(2, part2, in2, half2, out2, 7),
             1: basis,
-            3: coupling,
-            4: update,
+            3: lambda: reduce_c(2, half2, out2, g2, 8),
+            5: coupling,
+            6: update,
         },
     )
-    w1 = m[:, BLOCK:]
-    r11 = jnp.where(upper, m[:, :BLOCK], 0.0)
-    r1j = mm(w1, u1j[...])
-    rr[BLOCK:, :] = jnp.where(zero, 0.0, jnp.where(one, r11, r1j))
-
-    def tail(at):
-        q1 = mm(pan1[at, :], w1, 1, 1)
-        later = own[at, :] - mm(q1, r1j)
-        fac[at, :] = jnp.where(
-            zero, pan0[at, :] * stretch, jnp.where(one, q1 * stretch, later)
-        )
-
-    tiles(tail)
+    save(m, m_out, 4)
+    for copy in saved:
+        copy.wait()
     for copy in started:
         copy.wait_send()
     loop(lambda i: send_first(i).wait_send())
     loop(lambda i: send_second(i).wait_send())
     loop(lambda i: send_own(i).wait_send())
+
+
+def finish(
+    stretch, chunk, x1_any, x2_any, top_any, m_any, u_any, fac, rr, x1, x2, m, u1j, load
+):
+    pairs = [(m_any, m), (u_any, u1j), (x1_any, x1), (x2_any, x2), (top_any, rr.at[:BLOCK, :])]
+    loads = [pltpu.make_async_copy(a, b, load.at[k]) for k, (a, b) in enumerate(pairs)]
+    for copy in loads:
+        copy.start()
+    c = lax.axis_index("col")
+    zero, one = c == 0, c == 1
+    loads[0].wait()
+    loads[1].wait()
+    w1 = m[:, BLOCK:]
+    upper = lax.broadcasted_iota(jnp.int32, (BLOCK, BLOCK), 0) <= lax.broadcasted_iota(
+        jnp.int32, (BLOCK, BLOCK), 1
+    )
+    r1j = mm(w1, u1j[...])
+    r11 = jnp.where(upper, m[:, :BLOCK], 0.0)
+    rr[BLOCK:, :] = jnp.where(zero, 0.0, jnp.where(one, r11, r1j))
+
+    loads[2].wait()
+    loads[3].wait()
+
+    def tail(k, carry):
+        at = pl.ds(pl.multiple_of(k * chunk, chunk), chunk)
+        q1 = mm(x1[at, :], w1, 1, 1)
+        later = x2[at, :] - mm(q1, r1j)
+        fac[at, :] = jnp.where(zero, x2[at, :], jnp.where(one, q1 * stretch, later))
+        return carry
+
+    lax.fori_loop(0, x1.shape[0] // chunk, tail, 0)
+    loads[4].wait()
 
 
 def shards(n_col, n_row, jacobian, counts):
@@ -326,23 +369,37 @@
     staged = [
         buf(BLOCK, WIDE), buf(HALF, WIDE), buf(HALF, WIDE), buf(HALF, WIDE), buf(BLOCK, WIDE),
     ]
-    fac, rr = pl.pallas_call(
+    states = pl.pallas_call(
         functools.partial(kernel, n_col, stretch, chunk),
-        out_shape=(shape(local, BLOCK), shape(WIDE, BLOCK)),
+        out_shape=(
+            shape(local, BLOCK), shape(local, BLOCK), shape(BLOCK, BLOCK), shape(BLOCK, WIDE),
+            shape(BLOCK, BLOCK),
+        ),
         in_specs=[anywhere] * 2,
-        out_specs=(vmem,) * 2,
+        out_specs=(anywhere,) * 5,
         scratch_shapes=[
             buf(rows_dev, width), pltpu.VMEM((1, rows_dev), jnp.int32), buf(rows_dev, width),
             buf(local, BLOCK), buf(local, BLOCK), buf(local, BLOCK),
-            buf(BLOCK, BLOCK), buf(BLOCK, BLOCK), buf(BLOCK, BLOCK),
-            *staged, *staged, buf(BLOCK, WIDE), buf(BLOCK, BLOCK), buf(BLOCK, BLOCK),
-            pltpu.SemaphoreType.DMA((2,)), sems, sems, sems, sems, sems, sems,
+            buf(BLOCK, BLOCK), buf(PACK, BLOCK), buf(PACK, BLOCK), buf(PACK, BLOCK),
+            buf(BLOCK, BLOCK), *staged, *staged, buf(BLOCK, WIDE), buf(BLOCK, BLOCK), buf(BLOCK, BLOCK),
+            pltpu.SemaphoreType.DMA((2,)), pltpu.SemaphoreType.DMA((5,)), sems, sems, sems, sems, sems, sems,
             pltpu.SemaphoreType.DMA((9,)), pltpu.SemaphoreType.DMA((9,)),
         ],
         compiler_params=pltpu.CompilerParams(
             collective_id=0, has_side_effects=True, vmem_limit_bytes=56 * 1024 * 1024
         ),
     )(jacobian, counts.reshape(1, rows_dev))
+    fac, rr = pl.pallas_call(
+        functools.partial(finish, stretch, chunk),
+        out_shape=(shape(local, BLOCK), shape(WIDE, BLOCK)),
+        in_specs=[anywhere] * 5,
+        out_specs=(vmem,) * 2,
+        scratch_shapes=[
+            buf(local, BLOCK), buf(local, BLOCK), buf(BLOCK, WIDE), buf(BLOCK, BLOCK),
+            pltpu.SemaphoreType.DMA((5,)),
+        ],
+        compiler_params=pltpu.CompilerParams(vmem_limit_bytes=56 * 1024 * 1024),
+    )(*states)
     factored = fac.reshape(n_col, 1, rows_dev, 1, 1, BLOCK)
     return (factored, rr.reshape(WIDE, 1, 1, BLOCK))
 

time: 31.5 us -> 32.8 us (1.041)
  Pallas kernels: 28.4 us -> 32 us
  local copies, waits for them, and re-layouts: 2.26 us -> 0 us
    pallas_call x0 -> x1, Pallas kernels: none -> 2.5 us  [shards(): pl.pallas_call(functools.partial(finish, stretch, chunk), out_shape=(shap...]
    unnamed x4 -> x0, local copies, waits for them, and re-layouts: 2.26 us -> none
    pallas_call x1, Pallas kernels: 28.4 us -> 29.5 us  [shards(): pl.pallas_call(functools.partial(kernel, n_col, stretch, chunk), out_shap...]
where the time goes in v3:
time: 32.8 us; the launch traced here: 32.6 us
  Pallas kernels  32 us (98%)
  between operations  0.64 us (2%)
    pallas_call x1, Pallas kernels, shards(): pl.pallas_call(functools.partial(kernel, n_col, stretch, chunk), out_shap...  29.5 us
    pallas_call x1, Pallas kernels, shards(): pl.pallas_call(functools.partial(finish, stretch, chunk), out_shape=(shap...  2.5 us

profile of v3, /device:TPU:0, one launch (start us, length us, event | category | flops | bytes accessed | tf_op | source)
XLA Modules:
  0.0 32.6 jit_solution(3412532933983063313)
XLA Ops:
  0.6 29.5 %shard_map.41 = (f32[256,128]{1,0:T(8,128)}, f32[256,128]{1,0:T(8,128)}, f32[128,128]{1,0:T(8,128)}, f32[128,256]{1,0:T(8,128)}, f32[128,128]{1,0:T(8,128)}) custom-call(f32[32,1024]{1,0:T(8,128)} %jac_any.1, s32[1,32]{1,0:T(1,128)} %bitcast.7), custom_call_target="tpu_custom_call" | custom-call | tf_op jit(solution)/shard_map/pallas_call | solution.py:372
  30.1 2.5 %shard_map.42 = (f32[256,128]{1,0:T(8,128)}, f32[256,128]{1,0:T(8,128)}) custom-call(f32[256,128]{1,0:T(8,128)} %get-tuple-element.9.x1_any, f32[256,128]{1,0:T(8,128)} %get-tuple-element.10.x2_any, f32[128,128]{1,0:T(8,128)} %get-tuple-element.11.top_any, f32[128,256]{1,0:T(8,128)} %get-tuple-element.12.m_any, f32[128,128]{1,0:T(8,128)} %get-tuple-element.13.u_any), custom_call_target="tpu_custom_call" | custom-call | tf_op jit(solution)/shard_map/pallas_call | solution.py:392

commit v4 on v3

--- a/solution.py
+++ b/solution.py
@@ -156,6 +156,7 @@
     send_second = sender(pan1, send_p1, recv_p1, lambda t: pl.ds(BLOCK, BLOCK))
     send_own = sender(own, send_a, recv_a, block_of)
     loop(lambda i: send_first(i).start())
+    loop(lambda i: send_second(i).start())
     pan0[mine, :] = sc[:, :BLOCK]
     pan1[mine, :] = sc[:, BLOCK:WIDE]
     own[mine, :] = sc[:, block_of(c)]
@@ -202,7 +203,7 @@
         return copy
 
     loop(lambda i: send_first(i).wait_recv())
-    loop(lambda i: send_second(i).start())
+    loop(lambda i: send_own(i).start())
     gram(g0, first, pan0, pan0)
     low_lane = lax.broadcasted_iota(jnp.int32, (PACK - HALF, BLOCK), 1) < HALF
     pack[:HALF, :] = g0[:HALF, :]
@@ -233,7 +234,6 @@
     loop(lambda i: send_second(i).wait_recv())
     gram(part1, first, pan0, pan1)
     gram(part1, second, pan1, pan1)
-    loop(lambda i: send_own(i).start())
     reduce_a(1, part1, in1, 3)
     straight.wait_recv()
     slanted.wait_recv()
@@ -258,8 +258,9 @@
         m,
         {
             0: lambda: reduce_b(1, part1, in1, half1, out1, 5),
+            2: own_gram,
             4: lambda: reduce_c(1, half1, out1, g1, 6),
-            5: own_gram,
+            5: lambda: reduce_b(2, part2, in2, half2, out2, 7),
         },
     )
     w0 = m[:, BLOCK:]
@@ -305,11 +306,10 @@
     eliminate(
         m,
         {
-            0: lambda: reduce_b(2, part2, in2, half2, out2, 7),
+            0: lambda: reduce_c(2, half2, out2, g2, 8),
             1: basis,
-            3: lambda: reduce_c(2, half2, out2, g2, 8),
-            5: coupling,
-            6: update,
+            3: coupling,
+            4: update,
         },
     )
     save(m, m_out, 4)

time: 32.8 us -> 30.8 us (0.939)
  Pallas kernels: 32 us -> 30 us
    pallas_call x1, Pallas kernels: 29.5 us -> 27.5 us  [shards(): pl.pallas_call(functools.partial(kernel, n_col, stretch, chunk), out_shap...]
where the time goes in v4:
time: 30.8 us; the launch traced here: 30.6 us
  Pallas kernels  30 us (97%)
  between operations  0.64 us (2%)
    pallas_call x1, Pallas kernels, shards(): pl.pallas_call(functools.partial(kernel, n_col, stretch, chunk), out_shap...  27.5 us
    pallas_call x1, Pallas kernels, shards(): pl.pallas_call(functools.partial(finish, stretch, chunk), out_shape=(shap...  2.5 us

profile of v4, /device:TPU:0, one launch (start us, length us, event | category | flops | bytes accessed | tf_op | source)
XLA Modules:
  0.0 30.6 jit_solution(1705974795650587807)
XLA Ops:
  0.6 27.5 %shard_map.41 = (f32[256,128]{1,0:T(8,128)}, f32[256,128]{1,0:T(8,128)}, f32[128,128]{1,0:T(8,128)}, f32[128,256]{1,0:T(8,128)}, f32[128,128]{1,0:T(8,128)}) custom-call(f32[32,1024]{1,0:T(8,128)} %jac_any.1, s32[1,32]{1,0:T(1,128)} %bitcast.7), custom_call_target="tpu_custom_call" | custom-call | tf_op jit(solution)/shard_map/pallas_call | solution.py:372
  28.1 2.5 %shard_map.42 = (f32[256,128]{1,0:T(8,128)}, f32[256,128]{1,0:T(8,128)}) custom-call(f32[256,128]{1,0:T(8,128)} %get-tuple-element.9.x1_any, f32[256,128]{1,0:T(8,128)} %get-tuple-element.10.x2_any, f32[128,128]{1,0:T(8,128)} %get-tuple-element.11.top_any, f32[128,256]{1,0:T(8,128)} %get-tuple-element.12.m_any, f32[128,128]{1,0:T(8,128)} %get-tuple-element.13.u_any), custom_call_target="tpu_custom_call" | custom-call | tf_op jit(solution)/shard_map/pallas_call | solution.py:392
